TPU v7x, 32 devices: a whole 2x2x4 slice. The times are simulated.
32 devices in a mesh: dp: 8 (over z, y), row: 2 (over core), col: 2 (over x).
Axes of the slice: x: 2, y: 2, z: 4, core: 2. Of those that a mesh axis runs over, the one named last changes fastest.
Arguments:
- block_input: bfloat16 [4096, 2560], P(('dp', 'col')), may hold values from -6 to 6
- cotangent: bfloat16 [4096, 2560], P(('dp', 'col'), 'row'), may hold values from -6 to 6
- seq_lengths: int32 [32], replicated, may hold values from 16 to 128, as said below
- seq_owner: int32 [32], replicated, may hold values from 0 to 15, as said below
- norm_gain: bfloat16 [2560], P('row'), may hold values from 0.5 to 1.5
- proj_zx: bfloat16 [2560, 2, 5120], P('row', None, 'col'), may hold values from -0.125 to 0.125
- proj_bc: bfloat16 [2560, 256], P('row'), may hold values from -0.125 to 0.125
- proj_dt: bfloat16 [2560, 80], P('row', 'col'), may hold values from -0.125 to 0.125
- proj_out: bfloat16 [5120, 2560], P('col', 'row'), may hold values from -0.078125 to 0.078125
- inner_kernel: float32 [4, 5120], P(None, 'col'), may hold values from -3 to 3
- inner_offset: float32 [5120], P('col'), may hold values from -1.5 to 1.5
- shared_kernel: float32 [4, 256], replicated, may hold values from -3 to 3
- shared_offset: float32 [256], replicated, may hold values from -1.5 to 1.5
- decay_log: float32 [80], P('col'), may hold values from 0 to 2.77
- step_bias: float32 [80], P('col'), may hold values from -6 to -2
- skip_gain: float32 [80], P('col'), may hold values from 0.5 to 1.5
- output_gain: bfloat16 [5120], P('col'), may hold values from 0.5 to 1.5
Outputs:
- block_output: bfloat16 [4096, 2560], P(('dp', 'col'), 'row')
- input_grad: float32 [4096, 2560], P(('dp', 'col'), 'row')
- grad_norm: float32 [2560], P('row')
- grad_inproj: float32 [2560, 2, 5120], P('row', None, 'col')
- grad_shared: float32 [2560, 256], P('row')
- grad_steps: float32 [2560, 80], P('row', 'col')
- grad_outproj: float32 [5120, 2560], P('col', 'row')
- grad_kernel: float32 [4, 5120], P(None, 'col')
- grad_offset: float32 [5120], P('col')
- grad_skernel: float32 [4, 256], replicated
- grad_soffset: float32 [256], replicated
- grad_decay: float32 [80], P('col')
- grad_stepbias: float32 [80], P('col')
- grad_skip: float32 [80], P('col')
- grad_ogain: float32 [5120], P('col')
Inputs may be any that keep to these rules, and one draw needn't show every extreme that they name: `seq_lengths`: the lengths of the 2 sequences of one bucket sum to at most 256; in every draw some bucket holds 2 sequences of exactly 128 rows, so that its sum is 256. `seq_owner`: every bucket owns exactly 2 sequences.
All inputs are finite; a program needn't handle non-finite values.
Results may differ from a plain program's by a relative error of at most 0.0079.
The roundings to bfloat16 on the way count: a program that leaves them out, or rounds other values in their place, can miss the bound.
Values may be sent and summed in bfloat16 or wider, within the bound.
A program may use at most 256 MiB of HBM per device.

v0:
```python
import jax
import jax.numpy as jnp
from jax import lax
from jax.sharding import PartitionSpec as P

D = 2560
DI = 5120
SCAN_BLOCK = 256
CAP = 256


EPSILON = 1e-05
PRECISE = lax.Precision.HIGHEST


def layout(seq_lengths, seq_owner, bucket, capacity):
    owned = seq_owner == bucket
    owned_len = jnp.where(owned, seq_lengths, 0)
    starts = jnp.cumsum(owned_len) - owned_len
    places = jnp.arange(capacity, dtype=jnp.int32)[:, None]
    ends = starts + seq_lengths
    inside = owned[None, :] & (places >= starts[None, :]) & (places < ends[None, :])
    live_rows = jnp.any(inside, axis=1)
    seq_index = jnp.arange(seq_lengths.shape[0], dtype=jnp.int32)
    seq_ids = jnp.sum(jnp.where(inside, seq_index[None, :], 0), axis=1)
    seq_ids = jnp.where(live_rows, seq_ids, -1)
    return (seq_ids, live_rows.astype(jnp.float32))


def convolve(channels, kernel, offset, seq_ids, live_rows):
    tap_count = kernel.shape[0]
    summed_in = offset[None, :] + kernel[tap_count - 1][None, :] * channels
    for lag_steps in range(1, tap_count):
        lagged = jnp.concatenate(
            [jnp.zeros((lag_steps, channels.shape[1]), jnp.float32), channels[:-lag_steps]], axis=0
        )
        prior_ids = jnp.concatenate([jnp.full((lag_steps,), -1, jnp.int32), seq_ids[:-lag_steps]])
        same_seq = jnp.where((prior_ids == seq_ids) & (live_rows > 0), 1.0, 0.0).astype(jnp.float32)
        summed_in = (
            summed_in + kernel[tap_count - 1 - lag_steps][None, :] * lagged * same_seq[:, None]
        )
    return summed_in


def scan_blocks(
    values, inputs_b, inputs_c, step_sizes, decay_rate, skip_gain, seq_ids, live_rows, block_len
):
    rows_all, head_count, head_dim = values.shape
    state_size = inputs_b.shape[1]
    block_count = rows_all // block_len
    lower = jnp.arange(block_len)[:, None] >= jnp.arange(block_len)[None, :]

    def one_block(carried_in, block_item):
        memory, last_id = carried_in
        vals, bmat, cmat, sizes, rates, ids_here, live_here = block_item
        cumulated = jnp.cumsum(rates, axis=0)
        pair_live = (
            (ids_here[:, None] == ids_here[None, :])
            & (live_here[:, None] > 0)
            & (live_here[None, :] > 0)
            & lower
        )
        pair_mask = pair_live.astype(jnp.float32)
        scores = jnp.dot(cmat, bmat.T, precision=PRECISE)
        gap = jnp.where(pair_live[:, :, None], cumulated[:, None, :] - cumulated[None, :, :], 0.0)
        weights = jnp.exp(gap) * (pair_mask * scores)[:, :, None] * sizes[None, :, :]
        within = jnp.einsum("tsh,shp->thp", weights, vals, precision=PRECISE)
        carried = jnp.where((ids_here == last_id) & (live_here > 0), 1.0, 0.0).astype(jnp.float32)
        recalled = jnp.einsum("hpn,tn->thp", memory, cmat, precision=PRECISE)
        recalled = recalled * (jnp.exp(cumulated) * carried[:, None])[:, :, None]
        mixed_out = (within + recalled + skip_gain[None, :, None] * vals) * live_here[:, None, None]
        factor = jnp.exp(cumulated[-1][None, :] - cumulated) * pair_mask[-1][:, None] * sizes
        fresh_state = jnp.einsum("sh,shp,sn->hpn", factor, vals, bmat, precision=PRECISE)
        continues = jnp.where((ids_here[-1] == last_id) & (live_here[-1] > 0), 1.0, 0.0).astype(
            jnp.float32
        )
        memory = continues * jnp.exp(cumulated[-1])[:, None, None] * memory + fresh_state
        return ((memory, ids_here[-1]), mixed_out)

    items = (
        values.reshape(block_count, block_len, head_count, head_dim),
        inputs_b.reshape(block_count, block_len, state_size),
        inputs_c.reshape(block_count, block_len, state_size),
        step_sizes.reshape(block_count, block_len, head_count),
        decay_rate.reshape(block_count, block_len, head_count),
        seq_ids.reshape(block_count, block_len),
        live_rows.reshape(block_count, block_len),
    )
    start_state = (jnp.zeros((head_count, head_dim, state_size), jnp.float32), jnp.int32(-2))
    _, outputs = lax.scan(jax.checkpoint(one_block), start_state, items)
    return outputs.reshape(rows_all, head_count * head_dim)


def mixer_local(
    mixer_in,
    inner_kernel,
    inner_offset,
    shared_kernel,
    shared_offset,
    decay_log,
    step_bias,
    skip_gain,
    seq_ids,
    live_rows,
    block_len,
):
    inner_size = inner_kernel.shape[1]
    state_size = shared_kernel.shape[1] // 2
    head_count = decay_log.shape[0]
    gate_in = mixer_in[:, :inner_size]
    conv_in = mixer_in[:, inner_size : 2 * inner_size]
    shared_in = mixer_in[:, 2 * inner_size : 2 * inner_size + 2 * state_size]
    step_raw = mixer_in[:, 2 * inner_size + 2 * state_size :]
    mixed_x = jax.nn.silu(convolve(conv_in, inner_kernel, inner_offset, seq_ids, live_rows))
    mixed_bc = jax.nn.silu(convolve(shared_in, shared_kernel, shared_offset, seq_ids, live_rows))
    step_sizes = jax.nn.softplus(step_raw + step_bias[None, :])
    decay_rate = step_sizes * (-jnp.exp(decay_log))[None, :]
    values = mixed_x.reshape(mixed_x.shape[0], head_count, inner_size // head_count)
    ssm_out = scan_blocks(
        values,
        mixed_bc[:, :state_size],
        mixed_bc[:, state_size:],
        step_sizes,
        decay_rate,
        skip_gain,
        seq_ids,
        live_rows,
        block_len,
    )
    return ssm_out * jax.nn.silu(gate_in)


def per_device(
    block_input,
    cotangent,
    seq_lengths,
    seq_owner,
    norm_gain,
    proj_zx,
    proj_bc,
    proj_dt,
    proj_out,
    inner_kernel,
    inner_offset,
    shared_kernel,
    shared_offset,
    decay_log,
    step_bias,
    skip_gain,
    output_gain,
):
    row_count = lax.axis_size("row")
    col_count = lax.axis_size("col")
    row_index = lax.axis_index("row")
    col_index = lax.axis_index("col")
    data_index = lax.axis_index("dp")
    width_part = norm_gain.shape[0]
    inner_size = proj_zx.shape[2]
    state_size = proj_bc.shape[1] // 2
    tap_count = inner_kernel.shape[0]
    capacity = CAP
    bucket = data_index * row_count + row_index
    seq_ids, live_rows = layout(seq_lengths, seq_owner, bucket, capacity)
    rscale = lax.rsqrt(
        jnp.mean(jnp.square(block_input.astype(jnp.float32)), axis=1, keepdims=True) + EPSILON
    )
    own_cols = lax.dynamic_slice_in_dim(block_input, row_index * width_part, width_part, 1).astype(
        jnp.float32
    )
    normalized = own_cols * rscale
    gain_f = norm_gain.astype(jnp.float32)
    normed = (normalized * gain_f[None, :]).astype(jnp.bfloat16)
    normed_all = lax.all_gather(normed, "col", axis=0, tiled=True)
    weight_in = jnp.concatenate([proj_zx[:, 0, :], proj_zx[:, 1, :], proj_bc, proj_dt], axis=1)
    row_piece = normed_all
    mixer_in = lax.psum_scatter(
        jnp.dot(row_piece, weight_in, preferred_element_type=jnp.float32),
        "row",
        scatter_dimension=0,
        tiled=True,
    )

    def local_piece(
        mixer_value, kernel_a, offset_a, kernel_b, offset_b, decay_value, bias_value, skip_value
    ):
        return mixer_local(
            mixer_value,
            kernel_a,
            offset_a,
            kernel_b,
            offset_b,
            decay_value,
            bias_value,
            skip_value,
            seq_ids,
            live_rows,
            SCAN_BLOCK,
        )

    gated_rows, pull_back = jax.vjp(
        local_piece,
        mixer_in,
        inner_kernel,
        inner_offset,
        shared_kernel,
        shared_offset,
        decay_log,
        step_bias,
        skip_gain,
    )
    square_sum = lax.psum(jnp.sum(gated_rows * gated_rows, axis=1), "col")
    rnorm = lax.rsqrt(square_sum / DI + EPSILON)[:, None]
    out_gain = output_gain.astype(jnp.float32)
    branch = (gated_rows * rnorm * out_gain[None, :]).astype(jnp.bfloat16)
    branch_all = lax.all_gather(branch, "row", axis=0, tiled=True)
    row_piece = branch_all
    branch_out = lax.psum_scatter(
        jnp.dot(row_piece, proj_out, preferred_element_type=jnp.float32),
        "col",
        scatter_dimension=0,
        tiled=True,
    )
    block_output = (own_cols + branch_out).astype(jnp.bfloat16)
    cot_all = lax.all_gather(cotangent, "col", axis=0, tiled=True)
    row_piece = cot_all
    branch_grad = lax.psum_scatter(
        lax.dot_general(
            row_piece, proj_out, (((1,), (1,)), ((), ())), preferred_element_type=jnp.float32
        ),
        "row",
        scatter_dimension=0,
        tiled=True,
    )
    outproj_part = lax.dot_general(
        branch_all, cot_all, (((0,), (0,)), ((), ())), preferred_element_type=jnp.float32
    )
    outproj_total = outproj_part
    scaled_grad = branch_grad * out_gain[None, :]
    cross_sum = lax.psum(jnp.sum(scaled_grad * gated_rows, axis=1), "col")
    gated_grad = rnorm * scaled_grad - gated_rows * rnorm**3 * (cross_sum / DI)[:, None]
    ogain_part = jnp.sum(branch_grad * gated_rows * rnorm, axis=0)
    local_grads = pull_back(gated_grad)
    mixer_grad = local_grads[0].astype(jnp.bfloat16)
    mixer_all = lax.all_gather(mixer_grad, "row", axis=0, tiled=True)
    row_piece = mixer_all
    normed_grad = lax.psum_scatter(
        lax.dot_general(
            row_piece, weight_in, (((1,), (1,)), ((), ())), preferred_element_type=jnp.float32
        ),
        "col",
        scatter_dimension=0,
        tiled=True,
    )
    weight_grad = lax.dot_general(
        normed_all, mixer_all, (((0,), (0,)), ((), ())), preferred_element_type=jnp.float32
    )
    inproj_part = jnp.stack(
        [weight_grad[:, :inner_size], weight_grad[:, inner_size : 2 * inner_size]], axis=1
    )
    shared_part = weight_grad[:, 2 * inner_size : 2 * inner_size + 2 * state_size]
    steps_part = weight_grad[:, 2 * inner_size + 2 * state_size :]
    scaled_in = normed_grad * gain_f[None, :]
    norm_part = jnp.sum(normed_grad * normalized, axis=0)
    row_stat = lax.psum(jnp.sum(scaled_in * normalized, axis=1), "row")
    input_grad = cotangent.astype(jnp.float32) + rscale * (
        scaled_in - normalized * (row_stat / D)[:, None]
    )
    inproj_total, steps_total, outproj_total = lax.psum(
        (inproj_part, steps_part, outproj_total), "dp"
    )
    row_hot = (jnp.arange(row_count) == row_index).astype(jnp.float32)
    col_hot = (jnp.arange(col_count) == col_index).astype(jnp.float32)
    gain_slot = row_hot[:, None] * norm_part[None, :]
    shared_slot = row_hot[:, None, None] * shared_part[None, :, :]
    head_stack = jnp.stack([local_grads[5], local_grads[6], local_grads[7]], axis=0)
    head_slot = col_hot[None, :, None] * head_stack[:, None, :]
    chan_stack = jnp.concatenate(
        [local_grads[1], local_grads[2][None, :], ogain_part[None, :]], axis=0
    )
    chan_slot = col_hot[None, :, None] * chan_stack[:, None, :]
    shared_stack = jnp.concatenate([local_grads[3], local_grads[4][None, :]], axis=0)
    summed = lax.psum(
        (gain_slot, shared_slot, head_slot, chan_slot, shared_stack), ("dp", "row", "col")
    )
    gain_total = lax.dynamic_index_in_dim(summed[0], row_index, 0, keepdims=False)
    shared_total = lax.dynamic_index_in_dim(summed[1], row_index, 0, keepdims=False)
    head_total = lax.dynamic_index_in_dim(summed[2], col_index, 1, keepdims=False)
    chan_total = lax.dynamic_index_in_dim(summed[3], col_index, 1, keepdims=False)
    stack_total = summed[4]
    return (
        block_output,
        input_grad,
        gain_total,
        inproj_total,
        shared_total,
        steps_total,
        outproj_total,
        chan_total[:tap_count],
        chan_total[tap_count],
        stack_total[:tap_count],
        stack_total[tap_count],
        head_total[0],
        head_total[1],
        head_total[2],
        chan_total[tap_count + 1],
    )


def solution(mesh):
    return jax.shard_map(
        per_device,
        mesh=mesh,
        in_specs=(
            P(("dp", "col"), None),
            P(("dp", "col"), "row"),
            P(),
            P(),
            P("row"),
            P("row", None, "col"),
            P("row", None),
            P("row", "col"),
            P("col", "row"),
            P(None, "col"),
            P("col"),
            P(),
            P(),
            P("col"),
            P("col"),
            P("col"),
            P("col"),
        ),
        out_specs=(
            P(("dp", "col"), "row"),
            P(("dp", "col"), "row"),
            P("row"),
            P("row", None, "col"),
            P("row", None),
            P("row", "col"),
            P("col", "row"),
            P(None, "col"),
            P("col"),
            P(),
            P(),
            P("col"),
            P("col"),
            P("col"),
            P("col"),
        ),
        check_vma=False,
    )
```

profile of v0, /device:TPU:0, one launch (start us, length us, event | category | flops | bytes accessed | tf_op | source)
XLA Modules:
  0.0 1751.1 jit_solution(5665702625245222019)
XLA Ops:
  12.8 26.0 %fusion.116 = (bf16[1280,1,2560]{2,1,0:T(2,128)(2,1)S(1)}, bf16[1280,1,2560]{2,1,0:T(2,128)(2,1)}) fusion(bf16[1280,2,2560]{2,1,0:T(2,128)(2,1)} %param.22), kind=kLoop, calls=%fused_computation.231 | loop fusion | bytes 26214400 | tf_op jit(solution)/shard_map/slice | solution.py:174
  38.8 13.5 copy_bitcast_fusion
  52.3 18.4 %fusion.41 = f32[512,5416]{1,0:T(8,128)} fusion(bf16[512,1280]{1,0:T(8,128)(2,1)} %all-gather.5.cloned.1.call-done, bf16[1280,40]{1,0:T(8,128)(2,1)S(1)} %copy.146, bf16[1280,256]{1,0:T(8,128)(2,1)S(1)} %copy-done.88, bf16[1280,2560]{1,0:T(8,128)(2,1)} %get-tuple-element.342, bf16[1280,2560]{1,0:T(8,128)(2,1)} %get-tuple-element.343), kind=kOutput, calls=%fused_computation.76 | convolution fusion | flops 7154319360 | bytes 26267648 | tf_op jit(solution)/shard_map/dot_general | solution.py:177
  71.3 9.5 fusion.121
  84.9 8.7 reduce-scatter.5.cloned.1.call-done
  102.6 4.3 fusion.39
  116.1 11.7 fusion.5
  127.8 4.1 fusion.33
  134.0 4.0 multiply_reduce_fusion.10
  138.0 4.9 psum.77
  147.8 4.9 psum.78
  152.8 5.8 fusion.65
  169.7 7.2 multiply_reduce_fusion.2
  177.0 15.9 fusion.12
  198.8 6.1 fusion.69
  205.0 11.7 bitcast_add_fusion
  220.1 6.9 multiply_reduce_fusion.7
  227.0 4.0 multiply_reduce_fusion.6
  231.1 6.1 fusion.66
  257.2 15.5 all-gather.11.cloned.1.call-done
  272.7 17.4 fusion.122
  293.6 15.0 fusion.40
  308.7 8.9 fusion.120
  319.4 8.0 fusion.123
  329.0 14.7 slice_bitcast_fusion.1
  343.7 14.5 pad_maximum_fusion
  359.0 72.9 %all-reduce.36.cloned.1.call-done = (f32[2,1280,256]{2,1,0:T(8,128)}, f32[6,2,2560]{2,0,1:T(8,128)}) async-done(((f32[2,1280,256]{2,1,0:T(8,128)}, f32[6,2,2560]{2,0,1:T(8,128)}), (f32[2,1280,256]{2,1,0:T(8,128)}, f32[6,2,2560]{2,0,1:T(8,128)})) %all-reduce.36.cloned.1.call-update) | async-done | bytes 2744336 | tf_op jit(solution)/shard_map/psum | solution.py:282
  437.5 34.1 %reduce-scatter.11.cloned.1.call-done = f32[256,1280]{1,0:T(8,128)} async-done(((f32[512,1280]{1,0:T(8,128)}), f32[256,1280]{1,0:T(8,128)}) %reduce-scatter.11.cloned.1.call-update) | async-done | bytes 1310736 | tf_op jit(solution)/shard_map/reduce_scatter | solution.py:246
  473.6 40.0 %all-reduce.30 = (f32[2,1280]{1,0:T(2,128)S(1)}, f32[5,256]{1,0:T(8,128)S(1)}, f32[3,2,40]{2,1,0:T(2,128)S(1)}) all-reduce(f32[2,1280]{1,0:T(2,128)S(1)} %broadcast_multiply_fusion.9, f32[5,256]{1,0:T(8,128)S(1)} %pad_maximum_fusion.5, ...), channel_id=1, replica_groups=mesh['dp'=8,'row'=2,'col'=2] {'dp','row','col'}, use_global_device_ids=true, to_apply=%region_28.29 | all-reduce | flops 4080 | bytes 32640 | tf_op jit(solution)/shard_map/psum | solution.py:282
  521.5 1172.5 %all-reduce.38.cloned.1.call-done = (f32[1280,2,2560]{0,2,1:T(8,128)}, f32[1280,40]{0,1:T(8,128)}, f32[2560,1280]{1,0:T(8,128)}) async-done(((f32[1280,2,2560]{0,2,1:T(8,128)}, f32[1280,40]{0,1:T(8,128)}, f32[2560,1280]{1,0:T(8,128)}), (f32[1280,2,2560]{0,2,1:T(8,128)}, f32[1280,40]{0,1:T(8,128)}, f32[2560,1280]{1,0:T(8,128)})) %all-reduce.38.cloned.1.call-update) | async-done | bytes 39526416 | tf_op jit(solution)/shard_map/psum | solution.py:268
  1694.1 38.8 %copy.176 = f32[1280,2,2560]{2,1,0:T(2,128)} copy(f32[1280,2,2560]{0,2,1:T(8,128)} %get-tuple-element.270) | data formatting | bytes 52428800
  1733.5 10.5 copy.205
  (348 shorter events, 97.4 us)
Async XLA Ops:
  7.2 45.1 %all-gather.5.cloned.1.call-start = ((), (), s32[]{:S(2)}) async-start(), calls=%async_computation.4 | async-start | bytes 1966080 | tf_op jit(solution)/shard_map/all_gather | solution.py:173
  11.8 59.5 %all-gather.9.cloned.1.call-start = ((), (), s32[]{:S(2)}) async-start(), calls=%async_computation.8 | async-start | bytes 1966080 | tf_op jit(solution)/shard_map/all_gather | solution.py:224
  12.6 81.0 %reduce-scatter.5.cloned.1.call-start = ((), (), s32[]{:S(2)}) async-start(), calls=%async_computation.5 | async-start | bytes 16908288 | tf_op jit(solution)/shard_map/reduce_scatter | solution.py:176
  12.8 39.5 %copy-start.29 = (bf16[1280,40]{1,0:T(8,128)(2,1)}, bf16[1280,40]{1,0:T(8,128)(2,1)S(1)}, u32[]{:S(2)}) copy-start(bf16[1280,40]{1,0:T(8,128)(2,1)S(1)} %copy.146) | copy-start | bytes 307204
  70.8 73.2 %reduce-scatter.9.cloned.1.call-start = ((), (), s32[]{:S(2)}) async-start(), calls=%async_computation.9 | async-start | bytes 7864320 | tf_op jit(solution)/shard_map/reduce_scatter | solution.py:226
  80.9 191.8 %all-gather.11.cloned.1.call-start = ((), (), s32[]{:S(2)}) async-start(), calls=%async_computation.10 | async-start | bytes 8454144 | tf_op jit(solution)/shard_map/all_gather | solution.py:244
  82.8 18.7 %copy-start.37 = (f32[2560]{0:T(1024)}, f32[2560]{0:T(1024)S(1)}, u32[]{:S(2)}) copy-start(f32[2560]{0:T(1024)S(1)} %get-tuple-element.261) | copy-start | bytes 30724
  82.8 18.7 %copy-start.39 = (f32[2560]{0:T(1024)}, f32[2560]{0:T(1024)S(1)}, u32[]{:S(2)}) copy-start(f32[2560]{0:T(1024)S(1)} %get-tuple-element.263) | copy-start | bytes 30724
  82.8 18.7 %copy-start.41 = (f32[2560]{0:T(1024)}, f32[2560]{0:T(1024)S(1)}, u32[]{:S(2)}) copy-start(f32[2560]{0:T(1024)S(1)} %get-tuple-element.262) | copy-start | bytes 30724
  82.8 18.7 %copy-start.43 = (f32[2560]{0:T(1024)}, f32[2560]{0:T(1024)S(1)}, u32[]{:S(2)}) copy-start(f32[2560]{0:T(1024)S(1)} %get-tuple-element.264) | copy-start | bytes 30724
  82.9 15.3 copy-start.71
  82.9 44.8 %copy-start.52 = (f32[256]{0:T(256)}, f32[256]{0:T(256)S(1)}, u32[]{:S(2)}) copy-start(f32[256]{0:T(256)S(1)} %get-tuple-element.124) | copy-start | bytes 3076
  83.5 18.0 %copy-start.56 = (f32[256]{0:T(256)}, f32[256]{0:T(256)S(1)}, u32[]{:S(2)}) copy-start(f32[256]{0:T(256)S(1)} %get-tuple-element.335) | copy-start | bytes 3076
  83.5 18.0 %copy-start.59 = (f32[256]{0:T(256)}, f32[256]{0:T(256)S(1)}, u32[]{:S(2)}) copy-start(f32[256]{0:T(256)S(1)} %get-tuple-element.336) | copy-start | bytes 3076
  83.5 30.3 %copy-start.54 = (f32[256]{0:T(256)}, f32[256]{0:T(256)S(1)}, u32[]{:S(2)}) copy-start(f32[256]{0:T(256)S(1)} %get-tuple-element.334) | copy-start | bytes 3076
  95.4 17.4 copy-start.66
  109.4 18.4 %copy-start = (f32[256,2560]{0,1:T(8,128)}, f32[256,2560]{0,1:T(8,128)S(1)}, u32[]{:S(2)}) copy-start(f32[256,2560]{0,1:T(8,128)S(1)} %copy.149) | copy-start | bytes 7864324
  164.9 72.3 %copy-start.24 = (pred[256,256]{1,0:T(8,128)(4,1)}, pred[256,256]{1,0:T(8,128)(4,1)S(1)}, u32[]{:S(2)}) copy-start(pred[256,256]{1,0:T(8,128)(4,1)S(1)} %and_and_fusion) | copy-start | bytes 196612
  164.9 29.8 %copy-start.61 = (f32[1,256]{1,0:T(1,128)}, f32[1,256]{1,0:T(1,128)S(1)}, u32[]{:S(2)}) copy-start(f32[1,256]{1,0:T(1,128)S(1)} %slice_convert_fusion) | copy-start | bytes 3076
  192.8 44.4 %copy-start.26 = (f32[256,256]{1,0:T(8,128)}, f32[256,256]{1,0:T(8,128)S(1)}, u32[]{:S(2)}) copy-start(f32[256,256]{1,0:T(8,128)S(1)} %get-tuple-element.248) | copy-start | bytes 786436
  255.4 17.2 copy-start.87
  255.5 53.2 %all-gather.7.cloned.1.call-start = ((), (), s32[]{:S(2)}) async-start(), calls=%async_computation.6 | async-start | bytes 3932160 | tf_op jit(solution)/shard_map/all_gather | solution.py:215
  256.3 175.7 %all-reduce.36.cloned.1.call-start = ((), (), s32[]{:S(2)}) async-start(), calls=%async_computation.12 | async-start | bytes 5570560 | tf_op jit(solution)/shard_map/psum | solution.py:282
  293.6 178.1 %reduce-scatter.11.cloned.1.call-start = ((), (), s32[]{:S(2)}) async-start(), calls=%async_computation.11 | async-start | bytes 3932160 | tf_op jit(solution)/shard_map/reduce_scatter | solution.py:246
  308.7 209.8 %reduce-scatter.7.cloned.1.call-start = ((), (), s32[]{:S(2)}) async-start(), calls=%async_computation.7 | async-start | bytes 3932160 | tf_op jit(solution)/shard_map/reduce_scatter | solution.py:217
  317.6 1376.4 %all-reduce.38.cloned.1.call-start = ((), (), s32[]{:S(2)}) async-start(), calls=%async_computation.13 | async-start | bytes 79052800 | tf_op jit(solution)/shard_map/psum | solution.py:268
  358.3 113.4 %copy-start.16 = (bf16[256,2560]{1,0:T(8,128)(2,1)S(1)}, bf16[256,2560]{1,0:T(8,128)(2,1)}, u32[]{:S(2)}) copy-start(bf16[256,2560]{1,0:T(8,128)(2,1)} %param.17) | copy-start | bytes 3932164
  358.3 113.4 %copy-start.36 = (f32[1280]{0:T(1024)S(1)}, f32[1280]{0:T(1024)}, u32[]{:S(2)}) copy-start(f32[1280]{0:T(1024)} %copy-done.35) | copy-start | bytes 15364
  358.3 113.4 %copy-start.64 = (f32[256]{0:T(256)S(1)}, f32[256]{0:T(256)}, u32[]{:S(2)}) copy-start(f32[256]{0:T(256)} %copy-done.63) | copy-start | bytes 3076
  358.3 160.1 %copy-start.18 = (bf16[256,1280]{1,0:T(8,128)(2,1)S(1)}, bf16[256,1280]{1,0:T(8,128)(2,1)}, u32[]{:S(2)}) copy-start(bf16[256,1280]{1,0:T(8,128)(2,1)} %param.18) | copy-start | bytes 1966084
  471.7 46.8 %copy-start.17 = (f32[256,1280]{1,0:T(8,128)S(1)}, f32[256,1280]{1,0:T(8,128)}, u32[]{:S(2)}) copy-start(f32[256,1280]{1,0:T(8,128)} %reduce-scatter.11.cloned.1.call-done) | copy-start | bytes 3932164
  1694.1 38.8 %copy-start.34 = (f32[1280,40]{0,1:T(8,128)S(1)}, f32[1280,40]{0,1:T(8,128)}, u32[]{:S(2)}) copy-start(f32[1280,40]{0,1:T(8,128)} %get-tuple-element.349) | copy-start | bytes 614404
  (75 other events, 339.2 us)
Sparse Core Ops, SparseCore 0:
  11.9 26.9 all-gather.4
  40.4 24.2 all-gather.8
  70.9 22.6 reduce-scatter.4
  95.7 14.4 reduce-scatter.8
  255.6 17.0 all-gather.10
  274.7 12.5 all-gather.6
  294.3 137.5 all-reduce.35
  434.3 37.3 reduce-scatter.10
  473.9 38.2 reduce-scatter.6
  518.2 1175.8 all-reduce.37
where the time goes:
time: 1760 us; the launch traced here: 1750 us
  waiting for transfers between devices  1300 us (74%)
  local copies, waits for them, and re-layouts  152 us (9%)
  matrix products  145 us (8%)
  other arithmetic  78.9 us (4%)
  blocking collectives  52.3 us (3%)
    psum x1, waiting for transfers between devices, per_device(): lax.psum((inproj_part, steps_part, outproj_total), 'dp')  1170 us
    psum x1, waiting for transfers between devices, per_device(): lax.psum((gain_slot, shared_slot, head_slot, chan_slot, shared_stack), ('...  72.9 us
    unnamed x196, local copies, waits for them, and re-layouts  59.1 us
    psum x1, blocking collectives, per_device(): lax.psum((gain_slot, shared_slot, head_slot, chan_slot, shared_stack), ('...  40 us
    dot_general x3, matrix products, one_block(): within = jnp.einsum('tsh,shp->thp', weights, vals, precision=PRECISE)  39.3 us
  transfers between devices with their start and end apart: 10, of which 5 were waited for; matrix products, arithmetic and copies ran while one was open for 12% of the time, Pallas kernels for 0%

commit v1 on v0

v1 whole, which is shorter than its diff:
```python
import jax
import jax.numpy as jnp
from jax import lax
from jax.sharding import PartitionSpec as P

D = 2560
DI = 5120
CAP = 256


EPSILON = 1e-05
PRECISE = lax.Precision.HIGHEST


def layout(seq_lengths, seq_owner, bucket, capacity):
    owned = seq_owner == bucket
    owned_len = jnp.where(owned, seq_lengths, 0)
    order = jnp.arange(seq_lengths.shape[0], dtype=jnp.int32)
    starts = jnp.sum(jnp.where(order[None, :] < order[:, None], owned_len[None, :], 0), axis=1)
    places = jnp.arange(capacity, dtype=jnp.int32)[:, None]
    ends = starts + seq_lengths
    inside = owned[None, :] & (places >= starts[None, :]) & (places < ends[None, :])
    live_rows = jnp.any(inside, axis=1)
    seq_index = jnp.arange(seq_lengths.shape[0], dtype=jnp.int32)
    seq_ids = jnp.sum(jnp.where(inside, seq_index[None, :], 0), axis=1)
    seq_ids = jnp.where(live_rows, seq_ids, -1)
    return (seq_ids, live_rows.astype(jnp.float32))


def convolve(channels, kernel, offset, seq_ids, live_rows):
    tap_count = kernel.shape[0]
    summed_in = offset[None, :] + kernel[tap_count - 1][None, :] * channels
    for lag_steps in range(1, tap_count):
        lagged = jnp.concatenate(
            [jnp.zeros((lag_steps, channels.shape[1]), jnp.float32), channels[:-lag_steps]], axis=0
        )
        prior_ids = jnp.concatenate([jnp.full((lag_steps,), -1, jnp.int32), seq_ids[:-lag_steps]])
        same_seq = jnp.where((prior_ids == seq_ids) & (live_rows > 0), 1.0, 0.0).astype(jnp.float32)
        summed_in = (
            summed_in + kernel[tap_count - 1 - lag_steps][None, :] * lagged * same_seq[:, None]
        )
    return summed_in


def mix_bucket(values, bmat, cmat, sizes, rates, skip_gain, ids, live):
    rows_all, head_count, head_dim = values.shape
    lower = jnp.arange(rows_all)[:, None] >= jnp.arange(rows_all)[None, :]
    cumulated = jnp.dot(lower.astype(jnp.float32), rates, precision=PRECISE)
    pair_live = (
        (ids[:, None] == ids[None, :]) & (live[:, None] > 0) & (live[None, :] > 0) & lower
    )
    scores = jnp.dot(cmat, bmat.T, precision=PRECISE)
    gap = jnp.where(pair_live[:, :, None], cumulated[:, None, :] - cumulated[None, :, :], 0.0)
    weights = (
        jnp.exp(gap) * (pair_live.astype(jnp.float32) * scores)[:, :, None] * sizes[None, :, :]
    )
    within = jnp.einsum("tsh,shp->thp", weights, values, precision=PRECISE)
    mixed_out = (within + skip_gain[None, :, None] * values) * live[:, None, None]
    return mixed_out.reshape(rows_all, head_count * head_dim)


def sum_rows_over_dp(part, shared_cols=0):
    piece = lax.psum_scatter(
        part.astype(jnp.bfloat16), "dp", scatter_dimension=0, tiled=True
    )
    if shared_cols:
        own = piece.shape[1] - shared_cols
        tail = lax.psum(piece[:, own:].astype(jnp.float32), "col").astype(jnp.bfloat16)
        piece = jnp.concatenate([piece[:, :own], tail], axis=1)
    return lax.all_gather(piece, "dp", axis=0, tiled=True)


def mixer_local(
    conv_in,
    narrow_in,
    inner_kernel,
    inner_offset,
    shared_kernel,
    shared_offset,
    decay_log,
    step_bias,
    skip_gain,
    seq_ids,
    live_rows,
):
    inner_size = inner_kernel.shape[1]
    state_size = shared_kernel.shape[1] // 2
    head_count = decay_log.shape[0]
    shared_in = narrow_in[:, : 2 * state_size]
    step_raw = narrow_in[:, 2 * state_size :]
    mixed_x = jax.nn.silu(convolve(conv_in, inner_kernel, inner_offset, seq_ids, live_rows))
    mixed_bc = jax.nn.silu(convolve(shared_in, shared_kernel, shared_offset, seq_ids, live_rows))
    step_sizes = jax.nn.softplus(step_raw + step_bias[None, :])
    decay_rate = step_sizes * (-jnp.exp(decay_log))[None, :]
    values = mixed_x.reshape(mixed_x.shape[0], head_count, inner_size // head_count)
    return mix_bucket(
        values,
        mixed_bc[:, :state_size],
        mixed_bc[:, state_size:],
        step_sizes,
        decay_rate,
        skip_gain,
        seq_ids,
        live_rows,
    )


def per_device(
    block_input,
    cotangent,
    seq_lengths,
    seq_owner,
    norm_gain,
    proj_zx,
    proj_bc,
    proj_dt,
    proj_out,
    inner_kernel,
    inner_offset,
    shared_kernel,
    shared_offset,
    decay_log,
    step_bias,
    skip_gain,
    output_gain,
):
    row_count = lax.axis_size("row")
    col_count = lax.axis_size("col")
    row_index = lax.axis_index("row")
    col_index = lax.axis_index("col")
    data_index = lax.axis_index("dp")
    width_part = norm_gain.shape[0]
    inner_size = proj_zx.shape[2]
    state_size = proj_bc.shape[1] // 2
    tap_count = inner_kernel.shape[0]
    capacity = CAP
    bucket = data_index * row_count + row_index
    seq_ids, live_rows = layout(seq_lengths, seq_owner, bucket, capacity)
    rscale = lax.rsqrt(
        jnp.mean(jnp.square(block_input.astype(jnp.float32)), axis=1, keepdims=True) + EPSILON
    )
    own_cols = lax.dynamic_slice_in_dim(block_input, row_index * width_part, width_part, 1).astype(
        jnp.float32
    )
    normalized = own_cols * rscale
    gain_f = norm_gain.astype(jnp.float32)
    normed = (normalized * gain_f[None, :]).astype(jnp.bfloat16)
    normed_all = lax.all_gather(normed, "col", axis=0, tiled=True)
    weight_zx = proj_zx.reshape(width_part, 2 * inner_size)
    weight_narrow = jnp.concatenate([proj_bc, proj_dt], axis=1)
    zx_in = lax.psum_scatter(
        jnp.dot(normed_all, weight_zx, preferred_element_type=jnp.float32),
        "row",
        scatter_dimension=0,
        tiled=True,
    )
    narrow_in = lax.psum_scatter(
        jnp.dot(normed_all, weight_narrow, preferred_element_type=jnp.float32),
        "row",
        scatter_dimension=0,
        tiled=True,
    )
    gate_in = zx_in[:, :inner_size]
    conv_in = zx_in[:, inner_size:]

    def local_piece(*operands):
        return mixer_local(*operands, seq_ids, live_rows)

    ssm_rows, pull_back = jax.vjp(
        local_piece,
        conv_in,
        narrow_in,
        inner_kernel,
        inner_offset,
        shared_kernel,
        shared_offset,
        decay_log,
        step_bias,
        skip_gain,
    )
    gated_rows, gate_back = jax.vjp(
        lambda ssm_value, gate_value: ssm_value * jax.nn.silu(gate_value), ssm_rows, gate_in
    )
    square_sum = lax.psum(jnp.sum(gated_rows * gated_rows, axis=1), "col")
    rnorm = lax.rsqrt(square_sum / DI + EPSILON)[:, None]
    out_gain = output_gain.astype(jnp.float32)
    branch = (gated_rows * rnorm * out_gain[None, :]).astype(jnp.bfloat16)
    branch_all = lax.all_gather(branch, "row", axis=0, tiled=True)
    row_piece = branch_all
    branch_out = lax.psum_scatter(
        jnp.dot(row_piece, proj_out, preferred_element_type=jnp.float32),
        "col",
        scatter_dimension=0,
        tiled=True,
    )
    block_output = (own_cols + branch_out).astype(jnp.bfloat16)
    cot_all = lax.all_gather(cotangent, "col", axis=0, tiled=True)
    row_piece = cot_all
    branch_grad = lax.psum_scatter(
        lax.dot_general(
            row_piece, proj_out, (((1,), (1,)), ((), ())), preferred_element_type=jnp.float32
        ),
        "row",
        scatter_dimension=0,
        tiled=True,
    )
    outproj_part = lax.dot_general(
        branch_all, cot_all, (((0,), (0,)), ((), ())), preferred_element_type=jnp.float32
    )
    outproj_total = sum_rows_over_dp(outproj_part).astype(jnp.float32)
    scaled_grad = branch_grad * out_gain[None, :]
    cross_sum = lax.psum(jnp.sum(scaled_grad * gated_rows, axis=1), "col")
    gated_grad = rnorm * scaled_grad - gated_rows * rnorm**3 * (cross_sum / DI)[:, None]
    ogain_part = jnp.sum(branch_grad * gated_rows * rnorm, axis=0)
    ssm_grad, gate_grad = gate_back(gated_grad)
    gate_all = lax.all_gather(gate_grad.astype(jnp.bfloat16), "row", axis=0, tiled=True)
    gate_total = sum_rows_over_dp(
        lax.dot_general(
            normed_all, gate_all, (((0,), (0,)), ((), ())), preferred_element_type=jnp.float32
        )
    )
    local_grads = pull_back(ssm_grad)
    inner_all = lax.all_gather(
        local_grads[0].astype(jnp.bfloat16), "row", axis=0, tiled=True
    )
    narrow_all = lax.all_gather(
        local_grads[1].astype(jnp.bfloat16), "row", axis=0, tiled=True
    )
    normed_grad = lax.psum_scatter(
        lax.dot_general(
            jnp.concatenate([gate_all, inner_all], axis=1),
            weight_zx,
            (((1,), (1,)), ((), ())),
            preferred_element_type=jnp.float32,
        )
        + lax.dot_general(
            narrow_all, weight_narrow, (((1,), (1,)), ((), ())), preferred_element_type=jnp.float32
        ),
        "col",
        scatter_dimension=0,
        tiled=True,
    )
    inner_total = sum_rows_over_dp(
        lax.dot_general(
            normed_all, inner_all, (((0,), (0,)), ((), ())), preferred_element_type=jnp.float32
        )
    )
    narrow_part = lax.dot_general(
        normed_all, narrow_all, (((0,), (0,)), ((), ())), preferred_element_type=jnp.float32
    )
    narrow_total = sum_rows_over_dp(
        jnp.concatenate([narrow_part[:, 2 * state_size :], narrow_part[:, : 2 * state_size]], 1),
        2 * state_size,
    ).astype(jnp.float32)
    head_count = decay_log.shape[0]
    steps_total = narrow_total[:, :head_count]
    shared_total = narrow_total[:, head_count:]
    inproj_total = jnp.stack([gate_total, inner_total], axis=1).astype(jnp.float32)
    scaled_in = normed_grad * gain_f[None, :]
    norm_part = jnp.sum(normed_grad * normalized, axis=0)
    row_stat = lax.psum(jnp.sum(scaled_in * normalized, axis=1), "row")
    input_grad = cotangent.astype(jnp.float32) + rscale * (
        scaled_in - normalized * (row_stat / D)[:, None]
    )
    row_hot = (jnp.arange(row_count) == row_index).astype(jnp.float32)
    col_hot = (jnp.arange(col_count) == col_index).astype(jnp.float32)
    gain_slot = row_hot[:, None] * norm_part[None, :]
    head_stack = jnp.stack([local_grads[6], local_grads[7], local_grads[8]], axis=0)
    head_slot = col_hot[None, :, None] * head_stack[:, None, :]
    chan_stack = jnp.concatenate(
        [local_grads[2], local_grads[3][None, :], ogain_part[None, :]], axis=0
    )
    chan_slot = col_hot[None, :, None] * chan_stack[:, None, :]
    shared_stack = jnp.concatenate([local_grads[4], local_grads[5][None, :]], axis=0)
    summed = lax.psum(
        (gain_slot, head_slot, chan_slot, shared_stack), ("dp", "row", "col")
    )
    gain_total = lax.dynamic_index_in_dim(summed[0], row_index, 0, keepdims=False)
    head_total = lax.dynamic_index_in_dim(summed[1], col_index, 1, keepdims=False)
    chan_total = lax.dynamic_index_in_dim(summed[2], col_index, 1, keepdims=False)
    stack_total = summed[3]
    return (
        block_output,
        input_grad,
        gain_total,
        inproj_total,
        shared_total,
        steps_total,
        outproj_total,
        chan_total[:tap_count],
        chan_total[tap_count],
        stack_total[:tap_count],
        stack_total[tap_count],
        head_total[0],
        head_total[1],
        head_total[2],
        chan_total[tap_count + 1],
    )


def solution(mesh):
    return jax.shard_map(
        per_device,
        mesh=mesh,
        in_specs=(
            P(("dp", "col"), None),
            P(("dp", "col"), "row"),
            P(),
            P(),
            P("row"),
            P("row", None, "col"),
            P("row", None),
            P("row", "col"),
            P("col", "row"),
            P(None, "col"),
            P("col"),
            P(),
            P(),
            P("col"),
            P("col"),
            P("col"),
            P("col"),
        ),
        out_specs=(
            P(("dp", "col"), "row"),
            P(("dp", "col"), "row"),
            P("row"),
            P("row", None, "col"),
            P("row", None),
            P("row", "col"),
            P("col", "row"),
            P(None, "col"),
            P("col"),
            P(),
            P(),
            P("col"),
            P("col"),
            P("col"),
            P("col"),
        ),
        check_vma=False,
    )
```

time: 1760 us -> 1230 us (0.70)
  waiting for transfers between devices: 1300 us -> 837 us
  local copies, waits for them, and re-layouts: 152 us -> 92.1 us
  blocking collectives: 52.3 us -> 87.9 us
  matrix products: 145 us -> 124 us
    psum x2, waiting for transfers between devices: 1250 us -> 151 us  [the longest x1 128 us: per_device(): lax.psum((gain_slot, head_slot, chan_slot, shared_stack), ('dp', 'row', '...]
    reduce_scatter x2 -> x6, waiting for transfers between devices: 42.8 us -> 363 us  [the longest x3 344 us: sum_rows_over_dp(): lax.psum_scatter(part.astype(jnp.bfloat16), 'dp', scatter_dimension=0, ti...]
    all_gather x1 -> x5, waiting for transfers between devices: 15.5 us -> 243 us  [the longest x3 243 us: sum_rows_over_dp(): return lax.all_gather(piece, 'dp', axis=0, tiled=True)]
    unnamed x10 -> x20, waiting for transfers between devices: 0.84 us -> 56.6 us
    all_gather x0 -> x2, blocking collectives: none -> 35.2 us  [the longest x1 33 us: sum_rows_over_dp(): return lax.all_gather(piece, 'dp', axis=0, tiled=True)]
    slice x8 -> x7, local copies, waits for them, and re-layouts: 31.5 us -> 2.4 us  [the longest x1 1.31 us: per_device(): shared_total = narrow_total[:, head_count:]]
    convert_element_type x1 -> x3, other arithmetic: 1.69 us -> 23.2 us  [the longest x1 14.4 us: per_device(): jnp.stack([gate_total, inner_total], axis=1).astype(jnp.float32)]
    another operation x15 -> x2, other arithmetic: 19.7 us -> 0.02 us  [per_device(): jnp.stack([local_grads[6], local_grads[7], local_grads[8]], axis=0)]
  transfers between devices with their start and end apart: 10 -> 19, of which waited for: 5 -> 14; matrix products, arithmetic and copies ran while one was open for 12% -> 18% of each run, Pallas kernels for 0% -> 0%
where the time goes in v1:
time: 1230 us
  waiting for transfers between devices  837 us (68%)
  matrix products  124 us (10%)
  local copies, waits for them, and re-layouts  92.1 us (7%)
  blocking collectives  87.9 us (7%)
  other arithmetic  67.7 us (6%)
  between operations  15.3 us (1%)
    reduce_scatter x3, waiting for transfers between devices, sum_rows_over_dp(): lax.psum_scatter(part.astype(jnp.bfloat16), 'dp', scatter_dimension=0, ti...  344 us
    all_gather x3, waiting for transfers between devices, sum_rows_over_dp(): return lax.all_gather(piece, 'dp', axis=0, tiled=True)  243 us
    psum x1, waiting for transfers between devices, per_device(): lax.psum((gain_slot, head_slot, chan_slot, shared_stack), ('dp', 'row', '...  128 us
    unnamed x145, local copies, waits for them, and re-layouts  68.5 us
    unnamed x20, waiting for transfers between devices  56.6 us
    dot_general x3, matrix products, mix_bucket(): within = jnp.einsum('tsh,shp->thp', weights, values, precision=PRECISE)  45.8 us
    psum x1, blocking collectives, per_device(): lax.psum((gain_slot, head_slot, chan_slot, shared_stack), ('dp', 'row', '...  40.2 us
    all_gather x1, blocking collectives, sum_rows_over_dp(): return lax.all_gather(piece, 'dp', axis=0, tiled=True)  33 us
  transfers between devices with their start and end apart: 19, of which 14 were waited for; matrix products, arithmetic and copies ran while one was open for 18% of the time, Pallas kernels for 0%

profile of v1, /device:TPU:0, one launch (start us, length us, event | category | flops | bytes accessed | tf_op | source)
XLA Modules:
  0.0 1226.2 jit_solution(14746132511163028913)
XLA Ops:
  12.6 12.3 %copy.74 = bf16[160,8,2,2560]{3,1,2,0:T(8,128)(2,1)} copy(bf16[160,8,2,2560]{3,2,1,0:T(2,128)(2,1)} %bitcast.83) | data formatting | bytes 26214400
  25.1 13.7 %all-gather.9.cloned.1.call-done = bf16[512,1280]{1,0:T(8,128)(2,1)} async-done(((bf16[256,1280]{1,0:T(8,128)(2,1)}), bf16[512,1280]{1,0:T(8,128)(2,1)}) %all-gather.9.cloned.1.call-update) | async-done | bytes 1310736 | tf_op jit(solution)/shard_map/all_gather | solution.py:148
  41.8 12.3 %fusion.106 = f32[512,5120]{1,0:T(8,128)} fusion(bf16[512,1280]{1,0:T(8,128)(2,1)S(1)} %copy-done.17, bf16[1280,5120]{1,0:T(8,128)(2,1)} %bitcast.84), kind=kOutput, calls=%fused_computation.194 | convolution fusion | flops 6710886400 | bytes 24903680 | tf_op jit(solution)/shard_map/dot_general | solution.py:152
  54.2 10.5 all-gather.13.cloned.1.call-done
  64.7 9.2 fusion.108
  83.9 14.7 %reduce-scatter.12.cloned.1.call-done = f32[256,5120]{1,0:T(8,128)} async-done(((f32[512,5120]{1,0:T(8,128)}), f32[256,5120]{1,0:T(8,128)}) %reduce-scatter.12.cloned.1.call-update) | async-done | bytes 5242896 | tf_op jit(solution)/shard_map/reduce_scatter | solution.py:151
  110.1 15.6 %fusion.33 = f32[256,40,64]{0,2,1:T(8,128)} fusion(f32[256,40,64]{0,2,1:T(8,128)} %bitcast.88, f32[256,40]{0,1:T(8,128)S(1)} %compare_select_fusion.2, f32[256,256]{1,0:T(8,128)} %convolution_select_fusion, f32[256,40]{0,1:T(8,128)S(1)} %fusion.64, pred[256,256]{1,0:T(8,128)(4,1)S(1)} %fusion.65, f32[256]{0:T(256)S(1)} %get-tuple-element.145, ...), kind=kOutput, calls=%fused_computation.49 | convolution fusion | flops 2025717760 | bytes 5653664 | tf_op jit(solution)/shard_map/jvp(tsh,shp->thp)/dot_general | solution.py:57
  131.9 4.9 psum.56
  140.1 5.1 psum.57
  145.2 6.7 multiply_reduce_fusion.1
  154.2 11.6 bitcast_add_fusion
  182.6 18.6 %fusion.8 = (f32[256,40]{0,1:T(8,128)}, f32[256,40]{0,1:T(8,128)}, f32[256,40]{0,1:T(8,128)}, f32[256,256]{1,0:T(8,128)S(1)}) fusion(f32[256,40]{0,1:T(8,128)} %copy-done.31, f32[256,256]{1,0:T(8,128)} %convolution_select_fusion, f32[256,40]{0,1:T(8,128)} %copy-done.66, pred[256,256]{1,0:T(8,128)(4,1)S(1)} %fusion.65, f32[256,40,64]{0,2,1:T(8,128)S(1)} %bitcast.89, ...), kind=kOutput, calls=%fused_computation.15 | convolution fusion | flops 2047903744 | bytes 6038528 | tf_op jit(solution)/shard_map/transpose(jvp(tsh,shp->thp))/dot_general | solution.py:57
  210.6 7.3 convolution_convert_fusion.1
  218.0 7.6 convolution_convert_fusion.2
  226.9 8.0 convolution_convert_fusion
  236.6 55.0 %reduce-scatter.28.cloned.1.call-done = bf16[160,296]{1,0:T(8,128)(2,1)} async-done(((bf16[1280,296]{1,0:T(8,128)(2,1)}), bf16[160,296]{1,0:T(8,128)(2,1)}) %reduce-scatter.28.cloned.1.call-update) | async-done | bytes 94736
  293.5 13.9 %fusion.9 = f32[512,1280]{1,0:T(8,128)} fusion(bf16[1280,5120]{1,0:T(8,128)(2,1)} %bitcast.85, bf16[512,2560]{1,0:T(8,128)(2,1)} %all-gather.17.cloned.1.call-done, bf16[512,2560]{1,0:T(8,128)(2,1)} %all-gather.15.cloned.1.call-done), kind=kOutput, calls=%fused_computation.16 | convolution fusion | flops 6721372160 | bytes 20971520 | tf_op jit(solution)/shard_map/dot_general | solution.py:230
  307.3 4.1 convolution_add_fusion
  313.2 7.9 fusion.107
  321.2 95.2 %reduce-scatter.24.cloned.1.call-done = bf16[160,2560]{1,0:T(8,128)(2,1)} async-done(((bf16[1280,2560]{1,0:T(8,128)(2,1)}), bf16[160,2560]{1,0:T(8,128)(2,1)}) %reduce-scatter.24.cloned.1.call-update) | async-done | bytes 819216 | tf_op jit(solution)/shard_map/reduce_scatter | solution.py:63
  416.4 124.8 %reduce-scatter.22.cloned.1.call-done = bf16[160,2560]{1,0:T(8,128)(2,1)} async-done(((bf16[1280,2560]{1,0:T(8,128)(2,1)}), bf16[160,2560]{1,0:T(8,128)(2,1)}) %reduce-scatter.22.cloned.1.call-update) | async-done | bytes 819216 | tf_op jit(solution)/shard_map/reduce_scatter | solution.py:63
  541.3 124.2 %reduce-scatter.26.cloned.1.call-done = bf16[320,1280]{1,0:T(8,128)(2,1)} async-done(((bf16[2560,1280]{1,0:T(8,128)(2,1)}), bf16[320,1280]{1,0:T(8,128)(2,1)}) %reduce-scatter.26.cloned.1.call-update) | async-done | bytes 819216 | tf_op jit(solution)/shard_map/reduce_scatter | solution.py:63
  665.8 127.7 %all-reduce.32.cloned.1.call-done = f32[6,2,2560]{2,0,1:T(8,128)} async-done(((f32[6,2,2560]{2,0,1:T(8,128)}), f32[6,2,2560]{2,0,1:T(8,128)}) %all-reduce.32.cloned.1.call-update) | async-done | bytes 122896 | tf_op jit(solution)/shard_map/psum | solution.py:275
  796.7 23.0 %all-reduce.30.cloned.1.call-done = bf16[160,256]{0,1:T(8,128)(2,1)} async-done(((bf16[160,256]{0,1:T(8,128)(2,1)}), bf16[160,256]{0,1:T(8,128)(2,1)}) %all-reduce.30.cloned.1.call-update) | async-done | bytes 81936 | tf_op jit(solution)/shard_map/psum | solution.py:68
  820.8 33.0 %all_gather.38 = bf16[1280,296]{1,0:T(8,128)(2,1)S(1)} all-gather(bf16[160,296]{1,0:T(8,128)(2,1)S(1)} %copy.67), channel_id=1, replica_groups=mesh['dp'=8,'row'=2,'col'=2] {'dp'}, dimensions={0}, use_global_device_ids=true | all-gather | bytes 852480 | tf_op jit(solution)/shard_map/all_gather | solution.py:70
  862.1 40.2 %all-reduce.26 = (f32[2,1280]{1,0:T(2,128)S(1)}, f32[5,256]{1,0:T(8,128)S(1)}, f32[3,2,40]{2,1,0:T(2,128)S(1)}) all-reduce(f32[2,1280]{1,0:T(2,128)S(1)} %broadcast_multiply_fusion.7, f32[5,256]{1,0:T(8,128)S(1)} %pad_maximum_fusion.6, ...), channel_id=1, replica_groups=mesh['dp'=8,'row'=2,'col'=2] {'dp','row','col'}, use_global_device_ids=true, to_apply=%region_20.21 | all-reduce | flops 4080 | bytes 32640 | tf_op jit(solution)/shard_map/psum | solution.py:275
  910.2 94.9 %all-gather.21.cloned.1.call-done = bf16[1280,2560]{1,0:T(8,128)(2,1)} async-done(((bf16[160,2560]{1,0:T(8,128)(2,1)}), bf16[1280,2560]{1,0:T(8,128)(2,1)}) %all-gather.21.cloned.1.call-update) | async-done | bytes 6553616 | tf_op jit(solution)/shard_map/all_gather | solution.py:70
  1005.1 102.7 %all-gather.19.cloned.1.call-done = bf16[1280,2560]{1,0:T(8,128)(2,1)} async-done(((bf16[160,2560]{1,0:T(8,128)(2,1)}), bf16[1280,2560]{1,0:T(8,128)(2,1)}) %all-gather.19.cloned.1.call-update) | async-done | bytes 6553616 | tf_op jit(solution)/shard_map/all_gather | solution.py:70
  1107.8 14.4 %maximum_convert_fusion = f32[1280,2,2560]{2,0,1:T(8,128)} fusion(bf16[1280,1,2560]{2,0,1:T(8,128)(2,1)} %bitcast.86, bf16[1280,1,2560]{2,0,1:T(8,128)(2,1)} %bitcast.87), kind=kLoop, calls=%fused_computation | loop fusion | flops 13107200 | bytes 39321600 | tf_op jit(solution)/shard_map/convert_element_type | solution.py:258
  1122.1 43.6 %copy.68 = f32[1280,2,2560]{2,1,0:T(2,128)} copy(f32[1280,2,2560]{2,0,1:T(8,128)} %maximum_convert_fusion) | data formatting | bytes 52428800
  1165.7 44.9 %all-gather.23.cloned.1.call-done = bf16[2560,1280]{1,0:T(8,128)(2,1)} async-done(((bf16[320,1280]{1,0:T(8,128)(2,1)}), bf16[2560,1280]{1,0:T(8,128)(2,1)}) %all-gather.23.cloned.1.call-update) | async-done | bytes 6553616 | tf_op jit(solution)/shard_map/all_gather | solution.py:70
  1210.6 8.8 convert_element_type.112
  (283 shorter events, 94.5 us)
Async XLA Ops:
  7.2 31.7 %all-gather.9.cloned.1.call-start = ((), (), s32[]{:S(2)}) async-start(), calls=%async_computation.9 | async-start | bytes 1966080 | tf_op jit(solution)/shard_map/all_gather | solution.py:148
  11.8 53.0 %all-gather.13.cloned.1.call-start = ((), (), s32[]{:S(2)}) async-start(), calls=%async_computation.14 | async-start | bytes 1966080 | tf_op jit(solution)/shard_map/all_gather | solution.py:197
  12.5 63.1 %reduce-scatter.14.cloned.1.call-start = ((), (), s32[]{:S(2)}) async-start(), calls=%async_computation.11 | async-start | bytes 909312 | tf_op jit(solution)/shard_map/reduce_scatter | solution.py:157
  12.6 26.3 %copy-start.20 = (bf16[1280,256]{1,0:T(8,128)(2,1)S(1)}, bf16[1280,256]{1,0:T(8,128)(2,1)}, u32[]{:S(2)}) copy-start(bf16[1280,256]{1,0:T(8,128)(2,1)} %param.23) | copy-start | bytes 1966084
  25.1 29.0 %copy-start.15 = (bf16[1280,40]{1,0:T(8,128)(2,1)}, bf16[1280,40]{1,0:T(8,128)(2,1)S(1)}, u32[]{:S(2)}) copy-start(bf16[1280,40]{1,0:T(8,128)(2,1)S(1)} %copy.61) | copy-start | bytes 307204
  41.8 56.8 %reduce-scatter.12.cloned.1.call-start = ((), (), s32[]{:S(2)}) async-start(), calls=%async_computation.10 | async-start | bytes 15728640 | tf_op jit(solution)/shard_map/reduce_scatter | solution.py:151
  54.2 82.6 %reduce-scatter.18.cloned.1.call-start = ((), (), s32[]{:S(2)}) async-start(), calls=%async_computation.15 | async-start | bytes 7864320 | tf_op jit(solution)/shard_map/reduce_scatter | solution.py:199
  74.0 136.6 %all-gather.17.cloned.1.call-start = ((), (), s32[]{:S(2)}) async-start(), calls=%async_computation.17 | async-start | bytes 3932160 | tf_op jit(solution)/shard_map/all_gather | solution.py:223
  75.1 25.6 %copy-start.65 = (f32[40]{0:T(128)}, f32[40]{0:T(128)S(1)}, u32[]{:S(2)}) copy-start(f32[40]{0:T(128)S(1)} %exponential_negate_fusion) | copy-start | bytes 484
  75.1 79.0 %copy-start.53 = (f32[256]{0:T(256)}, f32[256]{0:T(256)S(1)}, u32[]{:S(2)}) copy-start(f32[256]{0:T(256)S(1)} %get-tuple-element.145) | copy-start | bytes 3076
  75.2 93.9 %copy-start.37 = (f32[256]{0:T(256)}, f32[256]{0:T(256)S(1)}, u32[]{:S(2)}) copy-start(f32[256]{0:T(256)S(1)} %get-tuple-element.142) | copy-start | bytes 3076
  75.2 98.0 %copy-start.33 = (f32[256]{0:T(256)}, f32[256]{0:T(256)S(1)}, u32[]{:S(2)}) copy-start(f32[256]{0:T(256)S(1)} %get-tuple-element.140) | copy-start | bytes 3076
  75.3 98.0 %copy-start.35 = (f32[256]{0:T(256)}, f32[256]{0:T(256)S(1)}, u32[]{:S(2)}) copy-start(f32[256]{0:T(256)S(1)} %get-tuple-element.141) | copy-start | bytes 3076
  79.6 74.6 %copy-start.31 = (f32[256,40]{0,1:T(8,128)}, f32[256,40]{0,1:T(8,128)S(1)}, u32[]{:S(2)}) copy-start(f32[256,40]{0,1:T(8,128)S(1)} %compare_select_fusion.2) | copy-start | bytes 122884
  79.9 74.3 %copy-start.66 = (f32[256,40]{0,1:T(8,128)}, f32[256,40]{0,1:T(8,128)S(1)}, u32[]{:S(2)}) copy-start(f32[256,40]{0,1:T(8,128)S(1)} %fusion.64) | copy-start | bytes 122884
  180.9 37.1 %all-gather.15.cloned.1.call-start = ((), (), s32[]{:S(2)}) async-start(), calls=%async_computation.16 | async-start | bytes 3932160 | tf_op jit(solution)/shard_map/all_gather | solution.py:216
  181.7 44.4 %all-gather.11.cloned.1.call-start = ((), (), s32[]{:S(2)}) async-start(), calls=%async_computation.12 | async-start | bytes 3932160 | tf_op jit(solution)/shard_map/all_gather | solution.py:188
  202.0 89.6 %reduce-scatter.28.cloned.1.call-start = ((), (), s32[]{:S(2)}) async-start(), calls=%async_computation.27 | async-start | bytes 1105920
  210.5 205.8 %reduce-scatter.24.cloned.1.call-start = ((), (), s32[]{:S(2)}) async-start(), calls=%async_computation.21 | async-start | bytes 7372800 | tf_op jit(solution)/shard_map/reduce_scatter | solution.py:63
  217.9 323.3 %reduce-scatter.22.cloned.1.call-start = ((), (), s32[]{:S(2)}) async-start(), calls=%async_computation.19 | async-start | bytes 7372800 | tf_op jit(solution)/shard_map/reduce_scatter | solution.py:63
  225.6 439.9 %reduce-scatter.26.cloned.1.call-start = ((), (), s32[]{:S(2)}) async-start(), calls=%async_computation.24 | async-start | bytes 7372800 | tf_op jit(solution)/shard_map/reduce_scatter | solution.py:63
  234.9 558.6 %all-reduce.32.cloned.1.call-start = ((), (), s32[]{:S(2)}) async-start(), calls=%async_computation.26 | async-start | bytes 327680 | tf_op jit(solution)/shard_map/psum | solution.py:275
  236.6 583.2 %all-reduce.30.cloned.1.call-start = ((), (), s32[]{:S(2)}) async-start(), calls=%async_computation.23 | async-start | bytes 262144 | tf_op jit(solution)/shard_map/psum | solution.py:68
  293.4 566.7 %reduce-scatter.20.cloned.1.call-start = ((), (), s32[]{:S(2)}) async-start(), calls=%async_computation.18 | async-start | bytes 3932160 | tf_op jit(solution)/shard_map/reduce_scatter | solution.py:229
  311.5 595.6 %reduce-scatter.16.cloned.1.call-start = ((), (), s32[]{:S(2)}) async-start(), calls=%async_computation.13 | async-start | bytes 3932160 | tf_op jit(solution)/shard_map/reduce_scatter | solution.py:190
  321.1 344.6 %copy-start.63 = (f32[40]{0:T(128)S(1)}, f32[40]{0:T(128)}, u32[]{:S(2)}) copy-start(f32[40]{0:T(128)} %param.30) | copy-start | bytes 484
  321.1 475.6 %slice-start.2 = ((bf16[160,296]{1,0:T(8,128)(2,1)}), bf16[160,40]{1,0:T(8,128)(2,1)S(1)}, s32[]{:S(2)}) async-start(bf16[160,296]{1,0:T(8,128)(2,1)} %reduce-scatter.28.cloned.1.call-done), calls=%async_computation.30 | async-start | bytes 81920 | tf_op jit(solution)/shard_map/slice | solution.py:69
  321.1 684.0 %all-gather.21.cloned.1.call-start = ((), (), s32[]{:S(2)}) async-start(), calls=%async_computation.22 | async-start | bytes 7372800 | tf_op jit(solution)/shard_map/all_gather | solution.py:70
  416.3 691.4 %all-gather.19.cloned.1.call-start = ((), (), s32[]{:S(2)}) async-start(), calls=%async_computation.20 | async-start | bytes 7372800 | tf_op jit(solution)/shard_map/all_gather | solution.py:70
  541.2 669.4 %all-gather.23.cloned.1.call-start = ((), (), s32[]{:S(2)}) async-start(), calls=%async_computation.25 | async-start | bytes 7372800 | tf_op jit(solution)/shard_map/all_gather | solution.py:70
  855.1 52.0 %copy-start.12 = (bf16[256,1280]{1,0:T(8,128)(2,1)S(1)}, bf16[256,1280]{1,0:T(8,128)(2,1)}, u32[]{:S(2)}) copy-start(bf16[256,1280]{1,0:T(8,128)(2,1)} %param.18) | copy-start | bytes 1966084
  860.1 47.0 %copy-start.9 = (f32[256,1280]{1,0:T(8,128)S(1)}, f32[256,1280]{1,0:T(8,128)}, u32[]{:S(2)}) copy-start(f32[256,1280]{1,0:T(8,128)} %reduce-scatter.20.cloned.1.call-done) | copy-start | bytes 3932164
  (57 other events, 365.3 us)
Sparse Core Ops, SparseCore 0:
  11.9 26.9 all-gather.8
  40.4 24.2 all-gather.12
  67.6 8.0 reduce-scatter.13
  78.4 20.1 reduce-scatter.11
  100.7 14.4 reduce-scatter.17
  181.0 12.5 all-gather.16
  195.8 12.6 all-gather.14
  210.8 12.5 all-gather.10
  227.1 64.4 reduce-scatter.27
  295.6 120.6 reduce-scatter.23
  420.4 120.7 reduce-scatter.21
  544.7 120.7 reduce-scatter.25
  672.5 120.9 all-reduce.31
  796.3 23.4 all-reduce.29
  822.5 37.5 reduce-scatter.19
  862.2 38.2 reduce-scatter.15
  902.8 102.2 all-gather.20
  1007.3 100.3 all-gather.18
  1110.2 100.3 all-gather.22

commit v2 on v1

--- a/solution.py
+++ b/solution.py
@@ -272,9 +272,14 @@
     )
     chan_slot = col_hot[None, :, None] * chan_stack[:, None, :]
     shared_stack = jnp.concatenate([local_grads[4], local_grads[5][None, :]], axis=0)
-    summed = lax.psum(
-        (gain_slot, head_slot, chan_slot, shared_stack), ("dp", "row", "col")
-    )
+    slots = (gain_slot, head_slot, chan_slot, shared_stack)
+    flat = lax.psum(
+        jnp.concatenate([slot.reshape(-1) for slot in slots]), ("dp", "row", "col")
+    )
+    summed, place = [], 0
+    for slot in slots:
+        summed.append(flat[place : place + slot.size].reshape(slot.shape))
+        place += slot.size
     gain_total = lax.dynamic_index_in_dim(summed[0], row_index, 0, keepdims=False)
     head_total = lax.dynamic_index_in_dim(summed[1], col_index, 1, keepdims=False)
     chan_total = lax.dynamic_index_in_dim(summed[2], col_index, 1, keepdims=False)

time: 1230 us -> 1230 us (level)
  blocking collectives: 87.9 us -> 47.8 us
  waiting for transfers between devices: 837 us -> 873 us
    psum x1 -> x0, blocking collectives: 40.2 us -> none  [per_device(): lax.psum((gain_slot, head_slot, chan_slot, shared_stack), ('dp', 'row', '...]
    reduce_scatter x3, waiting for transfers between devices: 344 us -> 373 us  [sum_rows_over_dp(): lax.psum_scatter(part.astype(jnp.bfloat16), 'dp', scatter_dimension=0, ti...]
    reduce_scatter x1, waiting for transfers between devices: 4.07 us -> 27.3 us  [per_device(): lax.psum_scatter(lax.dot_general(jnp.concatenate([gate_all, inner_all], a...]
    unnamed x20, waiting for transfers between devices: 56.6 us -> 39.3 us
    unnamed x145 -> x146, local copies, waits for them, and re-layouts: 68.5 us -> 67.8 us
  transfers between devices with their start and end apart: 19 -> 19, of which waited for: 14 -> 15; matrix products, arithmetic and copies ran while one was open for 18% -> 19% of each run, Pallas kernels for 0% -> 0%
where the time goes in v2:
time: 1230 us; the launch traced here: 1220 us
  waiting for transfers between devices  873 us (71%)
  matrix products  124 us (10%)
  local copies, waits for them, and re-layouts  94 us (8%)
  other arithmetic  68.3 us (6%)
  blocking collectives  47.8 us (4%)
  between operations  15.7 us (1%)
    reduce_scatter x3, waiting for transfers between devices, sum_rows_over_dp(): lax.psum_scatter(part.astype(jnp.bfloat16), 'dp', scatter_dimension=0, ti...  373 us
    all_gather x3, waiting for transfers between devices, sum_rows_over_dp(): return lax.all_gather(piece, 'dp', axis=0, tiled=True)  247 us
    psum x1, waiting for transfers between devices, per_device(): lax.psum(jnp.concatenate([slot.reshape(-1) for slot in slots]), ('dp', 'r...  123 us
    unnamed x146, local copies, waits for them, and re-layouts  67.8 us
    dot_general x3, matrix products, mix_bucket(): within = jnp.einsum('tsh,shp->thp', weights, values, precision=PRECISE)  45.8 us
    unnamed x20, waiting for transfers between devices  39.3 us
    all_gather x1, blocking collectives, sum_rows_over_dp(): return lax.all_gather(piece, 'dp', axis=0, tiled=True)  33 us
    reduce_scatter x1, waiting for transfers between devices, per_device(): lax.psum_scatter(lax.dot_general(jnp.concatenate([gate_all, inner_all], a...  27.3 us
  transfers between devices with their start and end apart: 19, of which 15 were waited for; matrix products, arithmetic and copies ran while one was open for 19% of the time, Pallas kernels for 0%

profile of v2, /device:TPU:0, one launch (start us, length us, event | category | flops | bytes accessed | tf_op | source)
XLA Modules:
  0.0 1224.7 jit_solution(16241338697541967064)
XLA Ops:
  12.6 12.3 %copy.75 = bf16[160,8,2,2560]{3,1,2,0:T(8,128)(2,1)} copy(bf16[160,8,2,2560]{3,2,1,0:T(2,128)(2,1)} %bitcast.83) | data formatting | bytes 26214400
  25.1 13.8 %all-gather.9.cloned.1.call-done = bf16[512,1280]{1,0:T(8,128)(2,1)} async-done(((bf16[256,1280]{1,0:T(8,128)(2,1)}), bf16[512,1280]{1,0:T(8,128)(2,1)}) %all-gather.9.cloned.1.call-update) | async-done | bytes 1310736 | tf_op jit(solution)/shard_map/all_gather | solution.py:148
  41.8 12.3 %fusion.106 = f32[512,5120]{1,0:T(8,128)} fusion(bf16[512,1280]{1,0:T(8,128)(2,1)S(1)} %copy-done.16, bf16[1280,5120]{1,0:T(8,128)(2,1)} %bitcast.84), kind=kOutput, calls=%fused_computation.195 | convolution fusion | flops 6710886400 | bytes 24903680 | tf_op jit(solution)/shard_map/dot_general | solution.py:152
  54.2 10.5 all-gather.13.cloned.1.call-done
  64.7 9.2 fusion.108
  83.8 14.8 %reduce-scatter.12.cloned.1.call-done = f32[256,5120]{1,0:T(8,128)} async-done(((f32[512,5120]{1,0:T(8,128)}), f32[256,5120]{1,0:T(8,128)}) %reduce-scatter.12.cloned.1.call-update) | async-done | bytes 5242896 | tf_op jit(solution)/shard_map/reduce_scatter | solution.py:151
  110.1 15.6 %fusion.33 = f32[256,40,64]{0,2,1:T(8,128)} fusion(f32[256,40,64]{0,2,1:T(8,128)} %bitcast.88, f32[256,40]{0,1:T(8,128)S(1)} %compare_select_fusion.2, f32[256,256]{1,0:T(8,128)} %convolution_select_fusion, f32[256,40]{0,1:T(8,128)S(1)} %fusion.64, pred[256,256]{1,0:T(8,128)(4,1)S(1)} %fusion.65, f32[256]{0:T(256)S(1)} %get-tuple-element.142, ...), kind=kOutput, calls=%fused_computation.49 | convolution fusion | flops 2025717760 | bytes 5653664 | tf_op jit(solution)/shard_map/jvp(tsh,shp->thp)/dot_general | solution.py:57
  131.9 4.9 psum.35
  140.1 5.1 psum.36
  145.2 7.4 multiply_reduce_fusion.6
  154.8 11.6 bitcast_add_fusion
  183.2 18.6 %fusion.8 = (f32[256,40]{0,1:T(8,128)}, f32[256,40]{0,1:T(8,128)}, f32[256,40]{0,1:T(8,128)}, f32[256,256]{1,0:T(8,128)S(1)}) fusion(f32[256,40]{0,1:T(8,128)} %copy-done.29, f32[256,256]{1,0:T(8,128)} %convolution_select_fusion, f32[256,40]{0,1:T(8,128)} %copy-done.66, pred[256,256]{1,0:T(8,128)(4,1)S(1)} %fusion.65, f32[256,40,64]{0,2,1:T(8,128)S(1)} %bitcast.89, ...), kind=kOutput, calls=%fused_computation.15 | convolution fusion | flops 2047903744 | bytes 6038528 | tf_op jit(solution)/shard_map/transpose(jvp(tsh,shp->thp))/dot_general | solution.py:57
  212.2 13.8 %fusion.9 = f32[512,1280]{1,0:T(8,128)} fusion(bf16[1280,5120]{1,0:T(8,128)(2,1)} %bitcast.85, bf16[512,2560]{1,0:T(8,128)(2,1)} %all-gather.17.cloned.1.call-done, bf16[512,2560]{1,0:T(8,128)(2,1)} %all-gather.15.cloned.1.call-done), kind=kOutput, calls=%fused_computation.16 | convolution fusion | flops 6721372160 | bytes 20971520 | tf_op jit(solution)/shard_map/dot_general | solution.py:230
  226.0 4.1 convolution_add_fusion
  230.4 7.3 convolution_convert_fusion.1
  237.8 7.3 convolution_convert_fusion.2
  246.4 8.0 convolution_convert_fusion
  254.5 37.6 %reduce-scatter.28.cloned.1.call-done = bf16[160,296]{1,0:T(8,128)(2,1)} async-done(((bf16[1280,296]{1,0:T(8,128)(2,1)}), bf16[160,296]{1,0:T(8,128)(2,1)}) %reduce-scatter.28.cloned.1.call-update) | async-done | bytes 94736
  293.9 7.9 fusion.107
  303.5 27.3 %reduce-scatter.20.cloned.1.call-done = f32[256,1280]{1,0:T(8,128)} async-done(((f32[512,1280]{1,0:T(8,128)}), f32[256,1280]{1,0:T(8,128)}) %reduce-scatter.20.cloned.1.call-update) | async-done | bytes 1310736 | tf_op jit(solution)/shard_map/reduce_scatter | solution.py:229
  333.5 123.6 %reduce-scatter.24.cloned.1.call-done = bf16[160,2560]{1,0:T(8,128)(2,1)} async-done(((bf16[1280,2560]{1,0:T(8,128)(2,1)}), bf16[160,2560]{1,0:T(8,128)(2,1)}) %reduce-scatter.24.cloned.1.call-update) | async-done | bytes 819216 | tf_op jit(solution)/shard_map/reduce_scatter | solution.py:63
  457.2 124.8 %reduce-scatter.22.cloned.1.call-done = bf16[160,2560]{1,0:T(8,128)(2,1)} async-done(((bf16[1280,2560]{1,0:T(8,128)(2,1)}), bf16[160,2560]{1,0:T(8,128)(2,1)}) %reduce-scatter.22.cloned.1.call-update) | async-done | bytes 819216 | tf_op jit(solution)/shard_map/reduce_scatter | solution.py:63
  582.0 124.8 %reduce-scatter.26.cloned.1.call-done = bf16[320,1280]{1,0:T(8,128)(2,1)} async-done(((bf16[2560,1280]{1,0:T(8,128)(2,1)}), bf16[320,1280]{1,0:T(8,128)(2,1)}) %reduce-scatter.26.cloned.1.call-update) | async-done | bytes 819216 | tf_op jit(solution)/shard_map/reduce_scatter | solution.py:63
  706.9 23.1 %all-reduce.31.cloned.1.call-done = bf16[160,256]{0,1:T(8,128)(2,1)} async-done(((bf16[160,256]{0,1:T(8,128)(2,1)}), bf16[160,256]{0,1:T(8,128)(2,1)}) %all-reduce.31.cloned.1.call-update) | async-done | bytes 81936 | tf_op jit(solution)/shard_map/psum | solution.py:68
  731.1 33.0 %all_gather.38 = bf16[1280,296]{1,0:T(8,128)(2,1)S(1)} all-gather(bf16[160,296]{1,0:T(8,128)(2,1)S(1)} %copy.67), channel_id=1, replica_groups=mesh['dp'=8,'row'=2,'col'=2] {'dp'}, dimensions={0}, use_global_device_ids=true | all-gather | bytes 852480 | tf_op jit(solution)/shard_map/all_gather | solution.py:70
  773.1 123.3 %all-reduce.29.cloned.1.call-done = f32[34800]{0:T(1024)} async-done(((f32[34800]{0:T(1024)}), f32[34800]{0:T(1024)}) %all-reduce.29.cloned.1.call-update) | async-done | bytes 139216 | tf_op jit(solution)/shard_map/psum | solution.py:276
  904.1 99.2 %all-gather.21.cloned.1.call-done = bf16[1280,2560]{1,0:T(8,128)(2,1)} async-done(((bf16[160,2560]{1,0:T(8,128)(2,1)}), bf16[1280,2560]{1,0:T(8,128)(2,1)}) %all-gather.21.cloned.1.call-update) | async-done | bytes 6553616 | tf_op jit(solution)/shard_map/all_gather | solution.py:70
  1003.2 102.7 %all-gather.19.cloned.1.call-done = bf16[1280,2560]{1,0:T(8,128)(2,1)} async-done(((bf16[160,2560]{1,0:T(8,128)(2,1)}), bf16[1280,2560]{1,0:T(8,128)(2,1)}) %all-gather.19.cloned.1.call-update) | async-done | bytes 6553616 | tf_op jit(solution)/shard_map/all_gather | solution.py:70
  1106.0 14.4 %maximum_convert_fusion = f32[1280,2,2560]{2,0,1:T(8,128)} fusion(bf16[1280,1,2560]{2,0,1:T(8,128)(2,1)} %bitcast.86, bf16[1280,1,2560]{2,0,1:T(8,128)(2,1)} %bitcast.87), kind=kLoop, calls=%fused_computation | loop fusion | flops 13107200 | bytes 39321600 | tf_op jit(solution)/shard_map/convert_element_type | solution.py:258
  1120.3 43.6 %copy.68 = f32[1280,2,2560]{2,1,0:T(2,128)} copy(f32[1280,2,2560]{2,0,1:T(8,128)} %maximum_convert_fusion) | data formatting | bytes 52428800
  1163.9 44.9 %all-gather.23.cloned.1.call-done = bf16[2560,1280]{1,0:T(8,128)(2,1)} async-done(((bf16[320,1280]{1,0:T(8,128)(2,1)}), bf16[2560,1280]{1,0:T(8,128)(2,1)}) %all-gather.23.cloned.1.call-update) | async-done | bytes 6553616 | tf_op jit(solution)/shard_map/all_gather | solution.py:70
  1208.8 8.8 convert_element_type.113
  (295 shorter events, 93.5 us)
Async XLA Ops:
  7.2 31.7 %all-gather.9.cloned.1.call-start = ((), (), s32[]{:S(2)}) async-start(), calls=%async_computation.9 | async-start | bytes 1966080 | tf_op jit(solution)/shard_map/all_gather | solution.py:148
  11.8 52.9 %all-gather.13.cloned.1.call-start = ((), (), s32[]{:S(2)}) async-start(), calls=%async_computation.14 | async-start | bytes 1966080 | tf_op jit(solution)/shard_map/all_gather | solution.py:197
  12.5 63.1 %reduce-scatter.14.cloned.1.call-start = ((), (), s32[]{:S(2)}) async-start(), calls=%async_computation.11 | async-start | bytes 909312 | tf_op jit(solution)/shard_map/reduce_scatter | solution.py:157
  12.6 26.3 %copy-start.19 = (bf16[1280,256]{1,0:T(8,128)(2,1)S(1)}, bf16[1280,256]{1,0:T(8,128)(2,1)}, u32[]{:S(2)}) copy-start(bf16[1280,256]{1,0:T(8,128)(2,1)} %param.23) | copy-start | bytes 1966084
  25.1 29.0 %copy-start.14 = (bf16[1280,40]{1,0:T(8,128)(2,1)}, bf16[1280,40]{1,0:T(8,128)(2,1)S(1)}, u32[]{:S(2)}) copy-start(bf16[1280,40]{1,0:T(8,128)(2,1)S(1)} %copy.61) | copy-start | bytes 307204
  41.8 56.8 %reduce-scatter.12.cloned.1.call-start = ((), (), s32[]{:S(2)}) async-start(), calls=%async_computation.10 | async-start | bytes 15728640 | tf_op jit(solution)/shard_map/reduce_scatter | solution.py:151
  54.2 82.6 %reduce-scatter.18.cloned.1.call-start = ((), (), s32[]{:S(2)}) async-start(), calls=%async_computation.15 | async-start | bytes 7864320 | tf_op jit(solution)/shard_map/reduce_scatter | solution.py:199
  74.0 138.2 %all-gather.17.cloned.1.call-start = ((), (), s32[]{:S(2)}) async-start(), calls=%async_computation.17 | async-start | bytes 3932160 | tf_op jit(solution)/shard_map/all_gather | solution.py:223
  75.1 25.6 %copy-start.65 = (f32[40]{0:T(128)}, f32[40]{0:T(128)S(1)}, u32[]{:S(2)}) copy-start(f32[40]{0:T(128)S(1)} %exponential_negate_fusion) | copy-start | bytes 484
  75.1 25.6 %copy-start.47 = (pred[256]{0:T(512)(128)(4,1)}, pred[256]{0:T(512)(128)(4,1)S(1)}, u32[]{:S(2)}) copy-start(pred[256]{0:T(512)(128)(4,1)S(1)} %get-tuple-element.143) | copy-start | bytes 772
  75.1 79.7 %copy-start.49 = (f32[256]{0:T(256)}, f32[256]{0:T(256)S(1)}, u32[]{:S(2)}) copy-start(f32[256]{0:T(256)S(1)} %get-tuple-element.142) | copy-start | bytes 3076
  75.2 94.6 %copy-start.33 = (f32[256]{0:T(256)}, f32[256]{0:T(256)S(1)}, u32[]{:S(2)}) copy-start(f32[256]{0:T(256)S(1)} %get-tuple-element.139) | copy-start | bytes 3076
  75.2 98.6 %copy-start.31 = (f32[256]{0:T(256)}, f32[256]{0:T(256)S(1)}, u32[]{:S(2)}) copy-start(f32[256]{0:T(256)S(1)} %get-tuple-element.138) | copy-start | bytes 3076
  79.5 75.2 %copy-start.29 = (f32[256,40]{0,1:T(8,128)}, f32[256,40]{0,1:T(8,128)S(1)}, u32[]{:S(2)}) copy-start(f32[256,40]{0,1:T(8,128)S(1)} %compare_select_fusion.2) | copy-start | bytes 122884
  79.8 75.0 %copy-start.66 = (f32[256,40]{0,1:T(8,128)}, f32[256,40]{0,1:T(8,128)S(1)}, u32[]{:S(2)}) copy-start(f32[256,40]{0,1:T(8,128)S(1)} %fusion.64) | copy-start | bytes 122884
  181.5 30.6 %all-gather.15.cloned.1.call-start = ((), (), s32[]{:S(2)}) async-start(), calls=%async_computation.16 | async-start | bytes 3932160 | tf_op jit(solution)/shard_map/all_gather | solution.py:216
  182.3 62.9 %all-gather.11.cloned.1.call-start = ((), (), s32[]{:S(2)}) async-start(), calls=%async_computation.12 | async-start | bytes 3932160 | tf_op jit(solution)/shard_map/all_gather | solution.py:188
  202.6 89.5 %reduce-scatter.28.cloned.1.call-start = ((), (), s32[]{:S(2)}) async-start(), calls=%async_computation.27 | async-start | bytes 1105920
  212.1 118.7 %reduce-scatter.20.cloned.1.call-start = ((), (), s32[]{:S(2)}) async-start(), calls=%async_computation.18 | async-start | bytes 3932160 | tf_op jit(solution)/shard_map/reduce_scatter | solution.py:229
  230.1 227.0 %reduce-scatter.24.cloned.1.call-start = ((), (), s32[]{:S(2)}) async-start(), calls=%async_computation.22 | async-start | bytes 7372800 | tf_op jit(solution)/shard_map/reduce_scatter | solution.py:63
  237.8 344.2 %reduce-scatter.22.cloned.1.call-start = ((), (), s32[]{:S(2)}) async-start(), calls=%async_computation.20 | async-start | bytes 7372800 | tf_op jit(solution)/shard_map/reduce_scatter | solution.py:63
  245.1 461.7 %reduce-scatter.26.cloned.1.call-start = ((), (), s32[]{:S(2)}) async-start(), calls=%async_computation.25 | async-start | bytes 7372800 | tf_op jit(solution)/shard_map/reduce_scatter | solution.py:63
  254.4 39.5 %copy-start.58 = (bf16[512,2560]{1,0:T(8,128)(2,1)S(1)}, bf16[512,2560]{1,0:T(8,128)(2,1)}, u32[]{:S(2)}) copy-start(bf16[512,2560]{1,0:T(8,128)(2,1)} %all-gather.11.cloned.1.call-done) | copy-start | bytes 7864324
  254.4 475.6 %all-reduce.31.cloned.1.call-start = ((), (), s32[]{:S(2)}) async-start(), calls=%async_computation.24 | async-start | bytes 262144 | tf_op jit(solution)/shard_map/psum | solution.py:68
  293.9 475.9 %reduce-scatter.16.cloned.1.call-start = ((), (), s32[]{:S(2)}) async-start(), calls=%async_computation.13 | async-start | bytes 3932160 | tf_op jit(solution)/shard_map/reduce_scatter | solution.py:190
  301.9 28.8 %copy-start.7 = (bf16[256,2560]{1,0:T(8,128)(2,1)S(1)}, bf16[256,2560]{1,0:T(8,128)(2,1)}, u32[]{:S(2)}) copy-start(bf16[256,2560]{1,0:T(8,128)(2,1)} %param.17) | copy-start | bytes 3932164
  301.9 28.8 %copy-start.36 = (f32[256]{0:T(256)S(1)}, f32[256]{0:T(256)}, u32[]{:S(2)}) copy-start(f32[256]{0:T(256)} %copy-done.35) | copy-start | bytes 3076
  302.0 594.4 %all-reduce.29.cloned.1.call-start = ((), (), s32[]{:S(2)}) async-start(), calls=%async_computation.19 | async-start | bytes 278528 | tf_op jit(solution)/shard_map/psum | solution.py:276
  303.3 403.5 %slice-start.2 = ((bf16[160,296]{1,0:T(8,128)(2,1)}), bf16[160,40]{1,0:T(8,128)(2,1)S(1)}, s32[]{:S(2)}) async-start(bf16[160,296]{1,0:T(8,128)(2,1)} %reduce-scatter.28.cloned.1.call-done), calls=%async_computation.30 | async-start | bytes 81920 | tf_op jit(solution)/shard_map/slice | solution.py:69
  333.4 669.8 %all-gather.21.cloned.1.call-start = ((), (), s32[]{:S(2)}) async-start(), calls=%async_computation.23 | async-start | bytes 7372800 | tf_op jit(solution)/shard_map/all_gather | solution.py:70
  457.1 648.8 %all-gather.19.cloned.1.call-start = ((), (), s32[]{:S(2)}) async-start(), calls=%async_computation.21 | async-start | bytes 7372800 | tf_op jit(solution)/shard_map/all_gather | solution.py:70
  582.0 626.8 %all-gather.23.cloned.1.call-start = ((), (), s32[]{:S(2)}) async-start(), calls=%async_computation.26 | async-start | bytes 7372800 | tf_op jit(solution)/shard_map/all_gather | solution.py:70
  (57 other events, 331.6 us)
Sparse Core Ops, SparseCore 0:
  11.9 26.9 all-gather.8
  40.4 24.2 all-gather.12
  67.6 8.0 reduce-scatter.13
  78.4 20.1 reduce-scatter.11
  100.7 14.4 reduce-scatter.17
  181.6 12.5 all-gather.16
  196.4 12.5 all-gather.14
  211.2 12.5 all-gather.10
  227.4 64.6 reduce-scatter.27
  294.2 36.5 reduce-scatter.19
  335.4 121.6 reduce-scatter.23
  461.1 120.7 reduce-scatter.21
  586.0 120.7 reduce-scatter.25
  709.5 20.5 all-reduce.30
  732.2 37.5 reduce-scatter.15
  776.1 120.1 all-reduce.28
  898.6 104.5 all-gather.20
  1005.5 100.3 all-gather.18
  1108.4 100.3 all-gather.22
